TPU v7x, 32 devices: a whole 2x2x4 slice. The times are simulated.
32 devices in a mesh: ka: 4 (over z), row: 2 (over x), col: 4 (over y, core).
Axes of the slice: x: 2, y: 2, z: 4, core: 2. Of those that a mesh axis runs over, the one named last changes fastest.
Arguments:
- screened_q: bfloat16 [2, 64, 2, 32, 20480], P(None, ('ka', 'row'), None, None, 'col'), may hold values from -48 to 48
- three_centre: bfloat16 [20480, 7168], P('col', 'row'), may hold values from -0.0390625 to 0.0390625
- green_fn: bfloat16 [2, 64, 112, 7168], P(None, 'ka', None, ('row', 'col')), may hold values from -0.0625 to 0.0625
- mask_three: int32 [128, 128], P('col', 'row'), may hold values 0 or 1
- mask_green: int32 [64, 2, 128], P('ka', None, ('row', 'col')), may hold values 0 or 1
- cell_list: int32 [64], replicated, may hold values from 0 to 63, each once
Outputs:
- sigma_window: float32 [2, 64, 32, 112], P(None, 'ka')
Inputs may be any that keep to these rules, and one draw needn't show every extreme that they name: `cell_list`: each of the 64 cell numbers appears once.
All inputs are finite; a program needn't handle non-finite values. No bound on the sum of `mask_three` or of `mask_green` on one device may be relied on, other than what follows from the above.
Results may differ from a plain program's by a relative error of at most 0.0041.
Values may be sent and summed in bfloat16 or wider, within the bound.
A program may use at most 192 MiB of HBM per device.

v0:
```python
import math

import jax
import jax.numpy as jnp
from jax import lax
from jax.sharding import PartitionSpec as P

KA = 8
KB = 8


def phase_table(cell_list, q_order):
    q_count = KA * KB
    q_first = q_order // KB
    q_second = q_order % KB
    cell_first = cell_list // KB
    cell_second = cell_list % KB
    phase_turns = (
        cell_first[:, None] * q_first[None, :] * KB + cell_second[:, None] * q_second[None, :] * KA
    ) % q_count
    angles = phase_turns.astype(jnp.float32) * (2.0 * math.pi / q_count)
    return (jnp.stack([jnp.cos(angles), -jnp.sin(angles)], axis=2) / q_count).astype(jnp.bfloat16)


def to_cells(block_in, phases):
    screened_cell = jnp.einsum(
        "rqc,tqcpa->trpa", phases, block_in, preferred_element_type=jnp.float32
    ).astype(jnp.bfloat16)
    return lax.all_to_all(screened_cell, "ka", split_axis=1, concat_axis=3, tiled=True)


def on_device(screened_q, three_centre, green_fn, mask_three, mask_green, cell_list):
    ka_count = lax.axis_size("ka")
    row_count = lax.axis_size("row")
    tau_count, q_local, planes, slab_rows, aux_local = screened_q.shape
    q_total = KA * KB
    pieces = screened_q.reshape(
        tau_count,
        q_local,
        planes,
        row_count,
        slab_rows // row_count,
        ka_count,
        aux_local // ka_count,
    )
    pieces = pieces.transpose(0, 1, 2, 5, 3, 4, 6).reshape(
        tau_count,
        q_local,
        planes,
        ka_count * row_count,
        slab_rows // row_count,
        aux_local // ka_count,
    )
    phases = phase_table(cell_list, jnp.arange(q_total, dtype=jnp.int32))
    screened_cell = to_cells(
        lax.all_to_all(pieces, ("ka", "row"), split_axis=3, concat_axis=1, tiled=True)[:, :, :, 0],
        phases,
    )
    aux_rows, orb_cols = three_centre.shape
    aux_blocks, orb_blocks = mask_three.shape
    row_keep = jnp.repeat(mask_three.astype(jnp.bfloat16), aux_rows // aux_blocks, axis=0)
    spread = (
        jnp.arange(orb_cols, dtype=jnp.int32)[None, :] // (orb_cols // orb_blocks)
        == jnp.arange(orb_blocks, dtype=jnp.int32)[:, None]
    ).astype(jnp.bfloat16)
    keep_three = jnp.dot(row_keep, spread, preferred_element_type=jnp.float32).astype(jnp.bfloat16)
    three_masked = three_centre * keep_three
    partial_mix = lax.dot_general(
        lax.all_gather(screened_cell, "row", axis=2, tiled=True),
        three_masked,
        (((3,), (0,)), ((), ())),
        preferred_element_type=jnp.float32,
    )
    mixed = lax.psum_scatter(partial_mix, "col", scatter_dimension=3, tiled=True).astype(
        jnp.bfloat16
    )
    block_width = green_fn.shape[3] // mask_green.shape[2]
    keep_green = jnp.repeat(
        jnp.repeat(mask_green.astype(jnp.bfloat16), block_width, axis=1), block_width, axis=2
    )
    green_masked = green_fn * keep_green[None]
    partial_sigma = jnp.einsum(
        "trpn,trmn->trpm", mixed, green_masked, preferred_element_type=jnp.float32
    )
    return lax.psum(partial_sigma, ("row", "col"))


def solution(mesh):
    return jax.shard_map(
        on_device,
        mesh=mesh,
        in_specs=(
            P(None, ("ka", "row"), None, None, "col"),
            P("col", "row"),
            P(None, "ka", None, ("row", "col")),
            P("col", "row"),
            P("ka", None, ("row", "col")),
            P(),
        ),
        out_specs=P(None, "ka", None, None),
        check_vma=False,
    )
```

profile of v0, /device:TPU:0, one launch (start us, length us, event | category | flops | bytes accessed | tf_op | source)
XLA Modules:
  0.0 776.5 jit_solution(6503558413168599353)
XLA Ops:
  6.5 19.3 %reshape.279 = bf16[2,8,2,2,16,4,1280]{6,5,4,3,2,1,0:T(4,128)(2,1)} reshape(bf16[2,8,2,32,5120]{4,3,2,1,0:T(8,128)(2,1)} %param.6) | data formatting | bytes 20971520 | tf_op jit(solution)/shard_map/reshape | solution.py:37
  25.9 13.8 %copy.12 = bf16[2,8,2,2,16,4,1280]{6,1,2,4,0,3,5:T(8,128)(2,1)} copy(bf16[2,8,2,2,16,4,1280]{6,5,4,3,2,1,0:T(4,128)(2,1)} %reshape.279) | data formatting | bytes 20971520 | tf_op jit(solution)/shard_map/reshape | solution.py:37
  39.7 7.4 all-to-all-start
  47.1 0.2 all-gather.2.cloned.1.call-start
  47.3 0.2 fusion.28
  47.6 227.6 %all-to-all-done = bf16[2,8,2,8,16,1280]{5,1,2,4,0,3:T(8,128)(2,1)} async-done(((bf16[2,8,2,8,16,1280]{5,1,2,4,0,3:T(8,128)(2,1)}), bf16[2,8,2,8,16,1280]{5,1,2,4,0,3:T(8,128)(2,1)}, u32[]{:S(2)}, u32[]{:S(2)}) %all-to-all-start) | async-done | bytes 10485792 | tf_op jit(solution)/shard_map/all_to_all | solution.py:56
  275.2 5.6 fusion.9
  280.8 2.9 copy.14
  283.7 119.1 %all_to_all.33 = bf16[2,64,16,1280]{3,2,0,1:T(8,128)(2,1)S(1)} all-to-all(bf16[2,64,16,1280]{3,2,0,1:T(8,128)(2,1)S(1)} %copy.14), channel_id=1, replica_groups=mesh['ka'=4,'row'=2,'col'=4] {'ka'}, dimensions={1} | all-to-all | bytes 10485760 | tf_op jit(solution)/shard_map/all_to_all | solution.py:29
  402.8 6.3 copy.33
  409.1 9.9 %all_to_all.30 = bf16[2,16,16,5120]{3,2,1,0:T(8,128)(2,1)} reshape(bf16[2,16,16,4,1280]{4,3,2,1,0:T(4,128)(2,1)} %bitcast.61) | data formatting | bytes 10485760 | tf_op jit(solution)/shard_map/all_to_all | solution.py:29
  419.0 0.0 all-gather.2.cloned.1.call-update
  419.0 0.0 copy-start
  419.0 0.3 reduce-scatter.2.cloned.1.call-start
  419.3 45.1 %copy.16 = bf16[5120,3584]{0,1:T(8,128)(2,1)} copy(bf16[5120,3584]{1,0:T(8,128)(2,1)} %param.7) | data formatting | bytes 73400320 | tf_op args[1]
  464.4 0.2 broadcast_in_dim.6
  464.6 25.3 %fusion.44 = bf16[5120,3584,1,1]{0,1,3,2:T(8,128)(2,1)} fusion(bf16[5120,3584]{0,1:T(8,128)(2,1)} %copy.16, bf16[5120,64]{1,0:T(8,128)(2,1)S(1)} %bitcast.63, s32[3584]{0:T(1024)S(1)} %add_select_fusion.1), kind=kOutput, calls=%fused_computation.2.clone.1 | convolution fusion | flops 2385969152 | bytes 74070016 | tf_op jit(solution)/shard_map/dot_general | solution.py:66
  489.8 57.3 %all-gather.2.cloned.1.call-done = bf16[2,16,32,5120]{3,2,1,0:T(8,128)(2,1)} async-done(((bf16[2,16,16,5120]{3,2,1,0:T(8,128)(2,1)}), bf16[2,16,32,5120]{3,2,1,0:T(8,128)(2,1)}) %all-gather.2.cloned.1.call-update) | async-done | bytes 10485776 | tf_op jit(solution)/shard_map/all_gather | solution.py:69
  547.1 46.2 %fusion = f32[2,16,32,3584]{3,2,1,0:T(8,128)} fusion(bf16[2,16,32,5120]{3,2,1,0:T(8,128)(2,1)} %all-gather.2.cloned.1.call-done, bf16[5120,3584,1,1]{0,1,3,2:T(8,128)(2,1)} %fusion.44), kind=kOutput, calls=%fused_computation.1 | convolution fusion | flops 37580963840 | bytes 61865984 | tf_op jit(solution)/shard_map/dot_general | solution.py:68
  593.3 0.0 reduce-scatter.2.cloned.1.call-update
  593.3 0.0 all-reduce.2.cloned.1.call-start
  593.4 0.6 copy-done.1
  594.0 0.2 copy.18
  594.2 0.3 broadcast_in_dim.7
  594.6 0.1 reshape.282
  594.7 2.3 broadcast_in_dim.8
  597.0 5.3 copy.19
  602.3 104.1 %reduce-scatter.2.cloned.1.call-done = f32[2,16,32,896]{3,2,1,0:T(8,128)} async-done(((f32[2,16,32,3584]{3,2,1,0:T(8,128)}), f32[2,16,32,896]{3,2,1,0:T(8,128)}) %reduce-scatter.2.cloned.1.call-update) | async-done | bytes 3670032 | tf_op jit(solution)/shard_map/reduce_scatter | solution.py:74
  706.4 6.9 fusion.5
  713.3 0.0 all-reduce.2.cloned.1.call-update
  713.3 54.7 %all-reduce.2.cloned.1.call-done = f32[2,16,32,112]{3,2,1,0:T(8,128)} async-done(((f32[2,16,32,112]{3,2,1,0:T(8,128)}), f32[2,16,32,112]{3,2,1,0:T(8,128)}) %all-reduce.2.cloned.1.call-update) | async-done | bytes 458768 | tf_op jit(solution)/shard_map/psum | solution.py:85
  768.1 1.9 copy.35
  (9 shorter events, 0.0 us)
Async XLA Ops:
  39.7 7.6 copy-start.2
  39.7 235.5 %all-to-all-start = ((bf16[2,8,2,8,16,1280]{5,1,2,4,0,3:T(8,128)(2,1)}), bf16[2,8,2,8,16,1280]{5,1,2,4,0,3:T(8,128)(2,1)}, u32[]{:S(2)}, u32[]{:S(2)}) async-start(bf16[2,8,2,8,16,1280]{5,1,2,4,0,3:T(8,128)(2,1)} %bitcast.59), calls=%async_computation | async-start | bytes 20971520 | tf_op jit(solution)/shard_map/all_to_all | solution.py:56
  47.1 500.0 %all-gather.2.cloned.1.call-start = ((), (), s32[]{:S(2)}) async-start(), calls=%async_computation.3 | async-start | bytes 15728640 | tf_op jit(solution)/shard_map/all_gather | solution.py:69
  419.0 45.3 %copy-start = (s32[32,64]{1,0:T(8,128)S(1)}, s32[32,64]{1,0:T(8,128)}, u32[]{:S(2)}) copy-start(s32[32,64]{1,0:T(8,128)} %param.9) | copy-start | bytes 24580
  419.0 287.4 %reduce-scatter.2.cloned.1.call-start = ((), (), s32[]{:S(2)}) async-start(), calls=%async_computation.4 | async-start | bytes 18350080 | tf_op jit(solution)/shard_map/reduce_scatter | solution.py:74
  593.3 0.7 copy-start.1
  593.3 174.7 %all-reduce.2.cloned.1.call-start = ((), (), s32[]{:S(2)}) async-start(), calls=%async_computation.5 | async-start | bytes 1048576 | tf_op jit(solution)/shard_map/psum | solution.py:85
Sparse Core Ops, SparseCore 0:
  419.1 127.9 all-gather.1
  593.4 112.9 reduce-scatter.1
  713.5 54.5 all-reduce.1
where the time goes:
time: 779 us; the launch traced here: 776 us
  waiting for transfers between devices  444 us (57%)
  blocking collectives  119 us (15%)
  local copies, waits for them, and re-layouts  108 us (14%)
  matrix products  83.9 us (11%)
  between operations  13.2 us (2%)
  starting transfers between devices  7.91 us (1%)
    all_to_all x1, waiting for transfers between devices, on_device(): lax.all_to_all(pieces, ('ka', 'row'), split_axis=3, concat_axis=1, tiled=...  228 us
    all_to_all x1, blocking collectives, to_cells(): lax.all_to_all(screened_cell, 'ka', split_axis=1, concat_axis=3, tiled=True)  119 us
    reduce_scatter x1, waiting for transfers between devices, on_device(): lax.psum_scatter(partial_mix, 'col', scatter_dimension=3, tiled=True)  104 us
    all_gather x1, waiting for transfers between devices, on_device(): lax.all_gather(screened_cell, 'row', axis=2, tiled=True)  57.3 us
    psum x1, waiting for transfers between devices, on_device(): return lax.psum(partial_sigma, ('row', 'col'))  54.7 us
    unnamed x8, local copies, waits for them, and re-layouts  47.6 us
    dot_general x1, matrix products, on_device(): lax.dot_general(lax.all_gather(screened_cell, 'row', axis=2, tiled=True),...  46.2 us
    reshape x2, local copies, waits for them, and re-layouts, on_device(): screened_q.reshape(tau_count, q_local, planes, row_count, slab_rows // ro...  33.2 us
  transfers between devices with their start and end apart: 4, of which 4 were waited for; matrix products, arithmetic and copies ran while one was open for 10% of the time, Pallas kernels for 0%

commit v1 on v0

v1 whole, which is shorter than its diff:
```python
import functools
import math

import jax
import jax.numpy as jnp
from jax import lax
from jax.experimental import pallas as pl
from jax.experimental.pallas import tpu as pltpu
from jax.sharding import PartitionSpec as P

KA = 8
KB = 8
P_PARTS = 2
LANES = 256
GREEN_CELLS = 4
VMEM_BYTES = 63 * 1024 * 1024


def phase_table(cell_list, q_order):
    q_count = KA * KB
    q_first = q_order // KB
    q_second = q_order % KB
    cell_first = cell_list // KB
    cell_second = cell_list % KB
    phase_turns = (
        cell_first[:, None] * q_first[None, :] * KB + cell_second[:, None] * q_second[None, :] * KA
    ) % q_count
    angles = phase_turns.astype(jnp.float32) * (2.0 * math.pi / q_count)
    return (jnp.stack([jnp.cos(angles), -jnp.sin(angles)], axis=2) / q_count).astype(jnp.bfloat16)


def two_terms(value):
    high = value.astype(jnp.bfloat16)
    return high, (value - high.astype(jnp.float32)).astype(jnp.bfloat16)


def remote(src, dst, send_sem, recv_sem, device_id):
    return pltpu.make_async_remote_copy(
        src_ref=src,
        dst_ref=dst,
        send_sem=send_sem,
        recv_sem=recv_sem,
        device_id=device_id,
        device_id_type=pl.DeviceIdType.MESH,
    )


def kernel(
    counts, share, by_part,
    x_ref, three_ref, green_ref, keep_three_ref, keep_green_ref, phase_ref,
    out_ref, land_ref,
    three, x_rows, parts, got_core, z_rows, send_y, got_y, send_z, got_z, own_z,
    green, sigma, got_sum, total, gathered,
    three_sem, row_sem, green_sem, x_send, x_recv, core_send, core_recv, y_send, y_recv,
    z_send, z_recv, sum_send, sum_recv, all_send, all_recv,
):
    ka_count, row_count, col_count = counts
    tau_count, q_local, planes, slab_rows, aux_local = x_ref.shape
    chunks, p_part = land_ref.shape[0], land_ref.shape[4]
    halves = chunks // tau_count
    rows = q_local * planes * p_part
    cells = keep_green_ref.shape[0]
    cell_groups = cells // GREEN_CELLS
    cell_rows = cells * p_part
    aux_blocks = keep_three_ref.shape[1]
    block = aux_local // aux_blocks
    n_part = three.shape[2]
    group = row_count * col_count
    ka, row, col = lax.axis_index("ka"), lax.axis_index("row"), lax.axis_index("col")
    place = row * col_count + col
    low_bit, high_bit = col % 2, col // 2
    core_peer = {"col": col + 1 - 2 * low_bit}
    y_peer = {"col": (col + 2) % 4}

    def member(step):
        other = (place + step) % group
        return other, {"row": other // col_count, "col": other % col_count}

    def three_copy(c):
        source = three_ref.at[c] if by_part else three_ref.at[:, pl.ds(c * n_part, n_part)]
        return pltpu.make_async_copy(source, three.at[c], three_sem.at[c])

    def green_copy(number):
        source = green_ref.at[
            number // (halves * cell_groups), pl.ds((number % cell_groups) * GREEN_CELLS, GREEN_CELLS)
        ]
        return pltpu.make_async_copy(source, green.at[number % 2], green_sem.at[number % 2])

    def own_rows(k):
        return x_ref.at[k // halves, :, :, pl.ds((k % halves) * p_part, p_part), :]

    def x_copy(k, s):
        return remote(
            own_rows(k), land_ref.at[k, s - 1], x_send.at[k, s - 1], x_recv.at[k, s - 1],
            {"row": (row + row_count - s) % row_count},
        )

    def core_copy(slot, j):
        return remote(
            parts.at[j], got_core.at[slot, j], core_send.at[j], core_recv.at[slot, j], core_peer
        )

    def y_copy(slot, s):
        return remote(send_y, got_y.at[slot, s], y_send, y_recv.at[slot, s], y_peer)

    def z_copy(slot, s):
        return remote(
            send_z.at[s - 1], got_z.at[slot, s - 1], z_send.at[s - 1], z_recv.at[slot, s - 1],
            {"ka": (ka + s) % ka_count},
        )

    for c in range(col_count):
        three_copy(c).start()
    for number in range(2):
        green_copy(number).start()

    barrier = pltpu.get_barrier_semaphore()
    for step in range(1, group):
        pl.semaphore_signal(
            barrier, inc=1, device_id=member(step)[1], device_id_type=pl.DeviceIdType.MESH
        )
    for step in range(1, ka_count):
        pl.semaphore_signal(
            barrier, inc=1, device_id={"ka": (ka + step) % ka_count},
            device_id_type=pl.DeviceIdType.MESH,
        )
    pl.semaphore_wait(barrier, group - 1 + ka_count - 1)

    for k in range(min(2, chunks)):
        for s in range(1, row_count):
            x_copy(k, s).start()

    for c in range(col_count):
        three_copy(c).wait()

    def mask_block(i, carry):
        c, b = i // aux_blocks, i % aux_blocks
        keep = keep_three_ref[c, pl.ds(b, 1), :].astype(jnp.bfloat16)
        here = pl.ds(pl.multiple_of(b * block, 16), block)
        three[c, here, :] = three[c, here, :] * keep
        return carry

    lax.fori_loop(0, col_count * aux_blocks, mask_block, 0)

    def unit(k, s):
        number = k * row_count + s
        slot = number % 2
        here = pl.ds(pl.multiple_of(s * rows, 8), rows)

        def multiply(o, carry):
            c = jnp.where(
                o < 2,
                2 * o + 1 - low_bit,
                2 * jnp.where(o == 2, 1 - high_bit, high_bit) + low_bit,
            )
            for first in range(0, n_part, LANES):
                lanes = slice(first, min(first + LANES, n_part))
                value = jnp.dot(
                    x_rows[...].reshape(rows, aux_local),
                    three[c, :, lanes],
                    preferred_element_type=jnp.float32,
                )

                @pl.when(o < 3)
                def _():
                    parts[jnp.minimum(o, 2), :, lanes] = value

                @pl.when(o == 3)
                def _():
                    z_rows[here, lanes] = value

            @pl.when(o < 2)
            def _():
                core_copy(slot, o).start()

            return carry

        lax.fori_loop(0, 4, multiply, 0)
        for j in range(2):
            core_copy(slot, j).wait_recv()

        @pl.when(number > 0)
        def _():
            y_copy(0, 0).wait_send()

        send_y[...] = (parts[2] + got_core[slot, 1 - high_bit]).astype(jnp.bfloat16)
        y_copy(k % 2, s).start()
        z_rows[here, :] += got_core[slot, high_bit]
        for j in range(2):
            core_copy(slot, j).wait_send()

    def finish(k):
        for s in range(1, ka_count):
            z_copy(k % 2, s).wait()

        def cell(r, carry):
            number = k * cell_groups + r // GREEN_CELLS

            @pl.when(r % GREEN_CELLS == 0)
            def _():
                green_copy(number).wait()

            here = pl.ds(pl.multiple_of(r * p_part, 16), p_part)
            mixed = own_z[here, :]
            for s in range(ka_count - 1):
                mixed = mixed + got_z[k % 2, s, here, :].astype(jnp.float32)
            lines = []
            for o in range(keep_green_ref.shape[1]):
                lines.extend(two_terms(mixed * keep_green_ref[r, o : o + 1, :]))
            both = lax.dot_general(
                jnp.concatenate(lines, axis=0),
                green[number % 2, r % GREEN_CELLS],
                (((1,), (1,)), ((), ())),
                preferred_element_type=jnp.float32,
            )
            width = both.shape[1] // keep_green_ref.shape[1]
            lane = lax.broadcasted_iota(jnp.int32, (p_part, both.shape[1]), 1) // width
            value = jnp.zeros((p_part, both.shape[1]), jnp.float32)
            for o in range(keep_green_ref.shape[1]):
                first = 2 * o * p_part
                summed = both[first : first + p_part] + both[first + p_part : first + 2 * p_part]
                value = jnp.where(lane == o, summed, value)
            sigma[pl.ds(pl.multiple_of(k * cell_rows + r * p_part, 8), p_part), :] = value

            @pl.when(
                jnp.logical_and(
                    r % GREEN_CELLS == GREEN_CELLS - 1, number + 2 < chunks * cell_groups
                )
            )
            def _():
                green_copy(number + 2).start()

            return carry

        lax.fori_loop(0, cells, cell, 0)

    def chunk(k, carry):
        load = pltpu.make_async_copy(own_rows(k), x_rows, row_sem)
        load.start()
        load.wait()
        unit(k, 0)

        @pl.when(k > 0)
        def _():
            finish(k - 1)

        def other_row(s, carry):
            x_copy(k, s).wait()

            @pl.when(k + 2 < chunks)
            def _():
                x_copy(k + 2, s).start()

            load = pltpu.make_async_copy(land_ref.at[k, s - 1], x_rows, row_sem)
            load.start()
            load.wait()
            unit(k, s)
            return carry

        lax.fori_loop(1, row_count, other_row, 0)

        for s in range(row_count):
            y_copy(k % 2, s).wait_recv()
            z_rows[s * rows : (s + 1) * rows, :] += got_y[k % 2, s].astype(jnp.float32)

        for first in range(0, n_part, LANES):
            lanes = slice(first, min(first + LANES, n_part))
            high, low = two_terms(z_rows[:, lanes])
            for s in range(ka_count):
                phases = phase_ref[s * cell_rows : (s + 1) * cell_rows, :]
                part = jnp.dot(phases, high, preferred_element_type=jnp.float32)
                part = part + jnp.dot(phases, low, preferred_element_type=jnp.float32)
                if s == 0:
                    own_z[:, lanes] = part
                else:
                    send_z[s - 1, :, lanes] = part.astype(jnp.bfloat16)
        for s in range(1, ka_count):
            z_copy(k % 2, s).start()
        return carry

    lax.fori_loop(0, chunks, chunk, 0)
    y_copy(0, 0).wait_send()
    finish(chunks - 1)

    if share == 0:
        out_ref[...] = sigma[...]
        return

    def sum_copy(step):
        other, device_id = member(step)
        return remote(
            sigma.at[pl.ds(pl.multiple_of(other * share, 8), share)], got_sum.at[step - 1],
            sum_send.at[step - 1], sum_recv.at[step - 1], device_id,
        )

    mine = pl.ds(pl.multiple_of(place * share, 8), share)

    def all_copy(step):
        return remote(
            total, gathered.at[mine], all_send.at[step - 1], all_recv.at[step - 1], member(step)[1]
        )

    for step in range(1, group):
        sum_copy(step).start()
    value = sigma[mine, :]
    for step in range(1, group):
        sum_copy(step).wait_recv()
        value = value + got_sum[step - 1]
    total[...] = value
    for step in range(1, group):
        all_copy(step).start()
    gathered[mine, :] = value
    for step in range(1, group):
        sum_copy(step).wait_send()
        all_copy(step).wait()
    out_ref[...] = gathered[...]


def on_device(screened_q, three_centre, green_fn, mask_three, mask_green, cell_list):
    counts = tuple(lax.axis_size(name) for name in ("ka", "row", "col"))
    ka_count, row_count, col_count = counts
    ka, row = lax.axis_index("ka"), lax.axis_index("row")
    tau_count, q_local, planes, slab_rows, aux_local = screened_q.shape
    orb_cols = three_centre.shape[1]
    n_part = orb_cols // col_count
    q_total = KA * KB
    cells = q_total // ka_count
    p_part = slab_rows // P_PARTS
    chunks = tau_count * P_PARTS
    rows = q_local * planes * p_part
    cell_rows = cells * p_part
    window = green_fn.shape[2]

    table = phase_table(jnp.roll(cell_list, -ka * cells), jnp.arange(q_total, dtype=jnp.int32))
    columns = [
        lax.dynamic_slice_in_dim(
            table, (ka * row_count + (row + s) % row_count) * q_local, q_local, axis=1
        )
        for s in range(row_count)
    ]
    phases = jnp.concatenate(columns, axis=1).reshape(q_total, row_count * q_local * planes)
    same = jnp.eye(p_part, dtype=jnp.bfloat16)
    phases = (phases[:, None, :, None] * same[None, :, None, :]).reshape(
        q_total * p_part, row_count * rows
    )

    keep_three = jnp.repeat(mask_three.astype(jnp.float32), orb_cols // mask_three.shape[1], axis=1)
    keep_three = keep_three.reshape(-1, col_count, n_part).transpose(1, 0, 2)
    keep_green = jnp.repeat(
        mask_green.astype(jnp.float32), green_fn.shape[3] // mask_green.shape[2], axis=2
    )
    by_part = n_part % 128 != 0
    if by_part:
        three_centre = three_centre.reshape(aux_local, col_count, n_part).transpose(1, 0, 2)

    group = row_count * col_count
    sigma_rows = chunks * cell_rows
    share = sigma_rows // group if sigma_rows % (8 * group) == 0 else 0
    any_space = pl.BlockSpec(memory_space=pl.ANY)
    vmem = pl.BlockSpec(memory_space=pltpu.VMEM)
    f32, bf16 = jnp.float32, jnp.bfloat16
    dma = pltpu.SemaphoreType.DMA
    sigma, _ = pl.pallas_call(
        functools.partial(kernel, counts, share, by_part),
        out_shape=(
            jax.ShapeDtypeStruct((sigma_rows, window), f32),
            jax.ShapeDtypeStruct(
                (chunks, row_count - 1, q_local, planes, p_part, aux_local), bf16
            ),
        ),
        in_specs=[any_space] * 3 + [vmem] * 3,
        out_specs=(vmem, any_space),
        scratch_shapes=[
            pltpu.VMEM((col_count, aux_local, n_part), bf16),
            pltpu.VMEM((q_local, planes, p_part, aux_local), bf16),
            pltpu.VMEM((3, rows, n_part), f32),
            pltpu.VMEM((2, 2, rows, n_part), f32),
            pltpu.VMEM((row_count * rows, n_part), f32),
            pltpu.VMEM((rows, n_part), bf16),
            pltpu.VMEM((2, row_count, rows, n_part), bf16),
            pltpu.VMEM((ka_count - 1, cell_rows, n_part), bf16),
            pltpu.VMEM((2, ka_count - 1, cell_rows, n_part), bf16),
            pltpu.VMEM((cell_rows, n_part), f32),
            pltpu.VMEM((2, GREEN_CELLS, window, n_part), bf16),
            pltpu.VMEM((sigma_rows, window), f32),
            pltpu.VMEM((group - 1, max(share, 8), window), f32),
            pltpu.VMEM((max(share, 8), window), f32),
            pltpu.VMEM((sigma_rows, window), f32),
            dma((col_count,)),
            dma,
            dma((2,)),
            dma((chunks, row_count - 1)),
            dma((chunks, row_count - 1)),
            dma((2,)),
            dma((2, 2)),
            dma,
            dma((2, row_count)),
            dma((ka_count - 1,)),
            dma((2, ka_count - 1)),
            dma((group - 1,)),
            dma((group - 1,)),
            dma((group - 1,)),
            dma((group - 1,)),
        ],
        compiler_params=pltpu.CompilerParams(
            collective_id=0, has_side_effects=True, vmem_limit_bytes=VMEM_BYTES
        ),
    )(screened_q, three_centre, green_fn, keep_three, keep_green, phases)
    sigma = sigma.reshape(tau_count, P_PARTS, cells, p_part, window)
    sigma = sigma.transpose(0, 2, 1, 3, 4).reshape(tau_count, cells, slab_rows, window)
    return sigma if share else lax.psum(sigma, ("row", "col"))


def solution(mesh):
    return jax.shard_map(
        on_device,
        mesh=mesh,
        in_specs=(
            P(None, ("ka", "row"), None, None, "col"),
            P("col", "row"),
            P(None, "ka", None, ("row", "col")),
            P("col", "row"),
            P("ka", None, ("row", "col")),
            P(),
        ),
        out_specs=P(None, "ka", None, None),
        check_vma=False,
    )
```

time: 779 us -> 433 us (0.56)
  waiting for transfers between devices: 444 us -> 0 us
  Pallas kernels: 0 us -> 398 us
  blocking collectives: 119 us -> 0 us
  local copies, waits for them, and re-layouts: 108 us -> 20.4 us
  matrix products: 83.9 us -> 0 us
  between operations: 13.2 us -> 0.07 us
  starting transfers between devices: 7.91 us -> 0 us
    pallas_call x0 -> x1, Pallas kernels: none -> 398 us  [on_device(): pl.pallas_call(functools.partial(kernel, counts, share, by_part), out_sha...]
    all_to_all x1 -> x0, waiting for transfers between devices: 228 us -> none  [on_device(): lax.all_to_all(pieces, ('ka', 'row'), split_axis=3, concat_axis=1, tiled=...]
    all_to_all x1 -> x0, blocking collectives: 119 us -> none  [to_cells(): lax.all_to_all(screened_cell, 'ka', split_axis=1, concat_axis=3, tiled=True)]
    reduce_scatter x1 -> x0, waiting for transfers between devices: 104 us -> none  [on_device(): lax.psum_scatter(partial_mix, 'col', scatter_dimension=3, tiled=True)]
    dot_general x4 -> x0, matrix products: 83.9 us -> none  [the longest x1 46.2 us: on_device(): lax.dot_general(lax.all_gather(screened_cell, 'row', axis=2, tiled=True),...]
    all_gather x1 -> x0, waiting for transfers between devices: 57.3 us -> none  [on_device(): lax.all_gather(screened_cell, 'row', axis=2, tiled=True)]
    psum x1 -> x0, waiting for transfers between devices: 54.7 us -> none  [on_device(): return lax.psum(partial_sigma, ('row', 'col'))]
    unnamed x8 -> x0, local copies, waits for them, and re-layouts: 47.6 us -> none
  transfers between devices with their start and end apart: 4 -> 0, of which waited for: 4 -> 0; matrix products, arithmetic and copies ran while one was open for 10% -> 0% of each run, Pallas kernels for 0% -> 0%
where the time goes in v1:
time: 433 us; the launch traced here: 425 us
  Pallas kernels  398 us (92%)
  local copies, waits for them, and re-layouts  20.4 us (5%)
  other arithmetic  6.49 us (1%)
    pallas_call x1, Pallas kernels, on_device(): pl.pallas_call(functools.partial(kernel, counts, share, by_part), out_sha...  398 us
    mul x2, local copies, waits for them, and re-layouts, on_device(): phases[:, None, :, None] * same[None, :, None, :]  15.2 us

profile of v1, /device:TPU:0, one launch (start us, length us, event | category | flops | bytes accessed | tf_op | source)
XLA Modules:
  0.0 424.5 jit_solution(1835790044147368978)
XLA Ops:
  0.0 0.8 pad_add_fusion
  0.8 0.1 and_select_fusion.3
  0.9 0.7 convert_element_type.30
  1.6 0.7 convert_element_type.31
  2.4 0.2 fusion.4
  2.6 0.1 constant_dynamic-slice_fusion.1
  2.7 0.1 pad_maximum_fusion
  2.8 0.1 copy.22
  2.9 0.1 copy.23
  3.0 0.1 broadcast_in_dim.5
  3.1 0.9 reshape.264.keep_green_ref
  4.0 0.3 broadcast_in_dim.4
  4.3 0.9 reshape_reshape.3
  5.3 0.8 copy.26
  6.1 3.8 broadcast_multiply_fusion
  9.9 15.1 %mul.118.phase_ref = bf16[1024,512]{1,0:T(8,128)(2,1)} reshape(bf16[64,16,32,16]{3,2,1,0:T(8,128)(2,1)} %broadcast_multiply_fusion) | data formatting | bytes 2097152 | tf_op jit(solution)/shard_map/mul | solution.py:343
  25.0 397.6 %shard_map.64 = (f32[1024,112]{1,0:T(8,128)}, bf16[4,1,8,2,16,5120]{5,4,3,2,1,0:T(8,128)(2,1)}) custom-call(bf16[2,8,2,32,5120]{4,3,2,1,0:T(8,128)(2,1)} %x_ref.1, bf16[5120,3584]{1,0:T(8,128)(2,1)} %three_ref.1, bf16[2,16,112,896]{3,2,1,0:T(8,128)(2,1)} %green_ref.1, f32[4,32,896]{2,1,0:T(8,128)} %bitcast.12, f32[16,2,896]{2,1,0:T(2,128)} %reshape.264.keep_green_ref, ...), custom_call_target="tpu_custom_call" | custom-call | tf_op jit(solution)/shard_map/pallas_call | solution.py:363
  422.6 1.9 copy.24
  (4 shorter events, 0.0 us)
